TPU v7x, 256 devices: a whole 4x4x8 slice. The times are simulated.
256 devices in a mesh: section: 32 (over z, x_hi, core), dp: 8 (over x_lo, y).
Axes of the slice: x: 4 (x_hi: 2, x_lo: 2; x = x_hi * 2 + x_lo), y: 4, z: 8, core: 2. Of those that a mesh axis runs over, the one named last changes fastest.
Arguments:
- inputs: bfloat16 [32, 1024, 6144], P('section', 'dp'), may hold values from -6 to 6
- stash: bfloat16 [32, 1024, 6144], P('section', 'dp'), may hold values from -6 to 6
- grad_in: bfloat16 [32, 1024, 6144], P('section', 'dp'), may hold values from -6 to 6
- proj: bfloat16 [32, 6144, 512], P('section', 'dp'), may hold values from -0.5 to 0.5
- gain: bfloat16 [32, 6144], P('section', 'dp'), may hold values from 0.099609375 to 1.8984375
- fwd_docs: int32 [32, 1024], P('section', 'dp'), may hold values from 0 to 63, never falling along the last dimension, each value on 1 to 64 neighbouring positions
- bwd_docs: int32 [32, 1024], P('section', 'dp'), may hold values from 0 to 63, never falling along the last dimension, each value on 1 to 64 neighbouring positions
Outputs:
- handed: bfloat16 [32, 1024, 6144], P('section', 'dp')
- returned: bfloat16 [32, 1024, 6144], P('section', 'dp')
- parked: bfloat16 [32, 1024, 6144], P('section', 'dp')
- proj_grad: bfloat16 [32, 6144, 512], P('section', 'dp')
- gain_grad: bfloat16 [32, 6144], P('section', 'dp')
Inputs may be any that keep to these rules, and one draw needn't show every extreme that they name: `fwd_docs`: document ids never fall along the tokens of a micro-batch; every id is used, no document is longer than 64 tokens, and one is exactly 64 long. Attention stays inside one data group's 128 tokens. `bwd_docs`: as for fwd_docs.
All inputs are finite; a program needn't handle non-finite values.
Results may differ from a plain program's by a relative error of at most 0.027.
Values may be sent and summed in bfloat16 or wider, within the bound.
A program may use at most 128 MiB of HBM per device.

v0:
```python
import jax
import jax.numpy as jnp
from jax import lax
from jax.sharding import PartitionSpec as P


def passed_along(block, axis, distance):
    devices = range(lax.axis_size(axis))
    route = [((i - distance) % len(devices), i) for i in devices]
    return lax.ppermute(block, axis, route)


def partner(value, axis, stride):
    mask = 2**stride
    pairs = [(source, source ^ mask) for source in range(lax.axis_size(axis))]
    return lax.ppermute(value, axis, pairs)


def passed_along_2(x, axis, by):
    peers = lax.axis_size(axis)
    pairs = [(i, i + by) for i in range(peers) if 0 <= i + by < peers]
    return lax.ppermute(x, axis, pairs)


def section_layer(activations, weights, norm_gain, doc_ids):
    head_size = weights.shape[1] // 4
    tok_count = activations.shape[0]
    width = activations.shape[1]
    head_count = width // head_size
    widened = activations.astype(jnp.float32)
    average = jnp.mean(widened, axis=-1, keepdims=True)
    centred = widened - average
    variance = jnp.mean(centred * centred, axis=-1, keepdims=True)
    normed = (centred * lax.rsqrt(variance + 1e-05) * norm_gain.astype(jnp.float32)).astype(
        jnp.bfloat16
    )
    blocks = normed.reshape(tok_count, head_count, head_size)
    in_maps = weights[:, : 3 * head_size].reshape(head_count, head_size, 3 * head_size)
    projected = jnp.einsum("thc,hce->the", blocks, in_maps, preferred_element_type=jnp.float32)
    queries = (projected[:, :, :head_size] * head_size ** (-0.5)).astype(jnp.bfloat16)
    key_rows = projected[:, :, head_size : 2 * head_size].astype(jnp.bfloat16)
    value_rows = projected[:, :, 2 * head_size :].astype(jnp.bfloat16)
    scores = jnp.einsum("thd,shd->hts", queries, key_rows, preferred_element_type=jnp.float32)
    row_ids = lax.broadcasted_iota(jnp.int32, (tok_count, tok_count), 0)
    col_ids = lax.broadcasted_iota(jnp.int32, (tok_count, tok_count), 1)
    allowed = (col_ids <= row_ids) & (doc_ids[:, None] == doc_ids[None, :])
    exp_scores = jnp.where(allowed[None], jnp.exp(scores), jnp.float32(0.0))
    attn_probs = (exp_scores / jnp.sum(exp_scores, axis=-1, keepdims=True)).astype(jnp.bfloat16)
    attended = jnp.einsum(
        "hts,shd->thd", attn_probs, value_rows, preferred_element_type=jnp.float32
    ).astype(jnp.bfloat16)
    out_maps = weights[:, 3 * head_size :].reshape(head_count, head_size, head_size)
    mixed = jnp.einsum(
        "thd,hcd->thc", attended, out_maps, preferred_element_type=jnp.float32
    ).reshape(tok_count, width)
    return (widened + mixed).astype(jnp.bfloat16)


def local(inputs, stash, grad_in, proj, gain, fwd_docs, bwd_docs):
    weights, gain_row = (
        lax.all_gather(proj[0], "dp", axis=0, tiled=True),
        lax.all_gather(gain[0], "dp", axis=0, tiled=True),
    )
    outgoing = section_layer(inputs[0], weights, gain_row, fwd_docs[0])
    handed = passed_along(outgoing, "section", 1)
    carried = (inputs[0], stash[0])
    for bit_index in range(lax.axis_size("section").bit_length() - 1):
        carried = partner((carried[0], carried[1]), "section", bit_index)
    parked, fetched = carried

    def local_layer(acts_in, weights_in, gain_in):
        return section_layer(acts_in, weights_in, gain_in, bwd_docs[0])

    unused, pullback = jax.vjp(local_layer, fetched, weights, gain_row)
    back_acts, weight_term, gain_term = pullback(grad_in[0])
    returned = passed_along_2(back_acts, "section", -1)
    groups = lax.axis_size("dp")
    summed = (
        lax.psum_scatter(
            weight_term.astype(jnp.float32).astype(jnp.bfloat16),
            "dp",
            scatter_dimension=0,
            tiled=True,
        ).astype(jnp.float32),
        lax.psum_scatter(
            gain_term.astype(jnp.float32).astype(jnp.bfloat16),
            "dp",
            scatter_dimension=0,
            tiled=True,
        ).astype(jnp.float32),
    )
    proj_grad = (summed[0] / groups).astype(jnp.bfloat16)
    gain_grad = (summed[1] / groups).astype(jnp.bfloat16)
    return (handed[None], returned[None], parked[None], proj_grad[None], gain_grad[None])


def solution(mesh):
    placed = (
        P("section", "dp", None),
        P("section", "dp", None),
        P("section", "dp", None),
        P("section", "dp", None),
        P("section", "dp"),
        P("section", "dp"),
        P("section", "dp"),
    )
    return jax.shard_map(
        local,
        mesh=mesh,
        in_specs=placed,
        out_specs=(
            P("section", "dp", None),
            P("section", "dp", None),
            P("section", "dp", None),
            P("section", "dp", None),
            P("section", "dp"),
        ),
        check_vma=False,
    )
```

profile of v0, /device:TPU:6, one launch (start us, length us, event | category | flops | bytes accessed | tf_op | source)
XLA Modules:
  0.0 531.2 jit_solution(5619902365384236365)
XLA Ops:
  8.1 3.6 collective-permute-done.1
  13.1 61.1 %collective-permute-done.2 = bf16[128,6144]{1,0:T(8,128)(2,1)S(1)} collective-permute-done((bf16[128,6144]{1,0:T(8,128)(2,1)S(1)}, bf16[128,6144]{1,0:T(8,128)(2,1)S(1)}, u32[]{:S(2)}, u32[]{:S(2)}) %collective-permute-start.2) | collective-permute-done | bytes 1572896 | tf_op jit(solution)/shard_map/ppermute | solution.py:16
  74.1 2.3 collective-permute-start.3
  76.4 32.4 %collective-permute-done.3 = bf16[128,6144]{1,0:T(8,128)(2,1)S(1)} collective-permute-done((bf16[128,6144]{1,0:T(8,128)(2,1)S(1)}, bf16[128,6144]{1,0:T(8,128)(2,1)S(1)}, u32[]{:S(2)}, u32[]{:S(2)}) %collective-permute-start.3) | collective-permute-done | bytes 1572896 | tf_op jit(solution)/shard_map/ppermute | solution.py:16
  108.8 4.3 collective-permute-start.4
  113.1 65.2 %collective-permute-done.4 = bf16[128,6144]{1,0:T(8,128)(2,1)S(1)} collective-permute-done((bf16[128,6144]{1,0:T(8,128)(2,1)S(1)}, bf16[128,6144]{1,0:T(8,128)(2,1)S(1)}, u32[]{:S(2)}, u32[]{:S(2)}) %collective-permute-start.4) | collective-permute-done | bytes 1572896 | tf_op jit(solution)/shard_map/ppermute | solution.py:16
  178.3 6.5 %collective-permute-start.5 = (bf16[128,6144]{1,0:T(8,128)(2,1)S(1)}, bf16[128,6144]{1,0:T(8,128)(2,1)S(1)}, u32[]{:S(2)}, u32[]{:S(2)}) collective-permute-start(bf16[128,6144]{1,0:T(8,128)(2,1)S(1)} %collective-permute-done.4), channel_id=1, source_target_pairs={{0,128},{8,136},{16,144},{24,152},{32,160},{40,168},{48,176},{56,1... | collective-permute-start | bytes 4718600 | tf_op jit(solution)/shard_map/ppermute | solution.py:16
  184.8 28.4 %all-gather = bf16[1,6144]{1,0:T(2,128)(2,1)S(1)} all-gather(bf16[1,768]{1,0:T(2,128)(2,1)} %param.11), channel_id=2, replica_groups=mesh['section'=32,'dp'=8] {'dp'}, dimensions={1}, use_global_device_ids=true | all-gather | bytes 13824 | tf_op jit(solution)/shard_map/all_gather | solution.py:62
  213.2 2.6 copy.41
  216.4 35.9 %collective-permute-done.5 = bf16[128,6144]{1,0:T(8,128)(2,1)S(1)} collective-permute-done((bf16[128,6144]{1,0:T(8,128)(2,1)S(1)}, bf16[128,6144]{1,0:T(8,128)(2,1)S(1)}, u32[]{:S(2)}, u32[]{:S(2)}) %collective-permute-start.5) | collective-permute-done | bytes 1572896 | tf_op jit(solution)/shard_map/ppermute | solution.py:16
  258.3 3.4 slice.38
  264.0 3.6 copy-done.3
  267.6 2.9 fusion.37
  272.4 5.3 convolution_convert_fusion
  277.7 3.7 fusion.64
  283.8 3.3 fusion.65
  291.0 3.2 pad_add_fusion.1
  294.6 34.6 %collective-permute-done.9 = bf16[128,6144]{1,0:T(8,128)(2,1)S(1)} collective-permute-done((bf16[128,6144]{1,0:T(8,128)(2,1)}, bf16[128,6144]{1,0:T(8,128)(2,1)S(1)}, u32[]{:S(2)}, u32[]{:S(2)}) %collective-permute-start.9) | collective-permute-done | bytes 1572896 | tf_op jit(solution)/shard_map/ppermute | solution.py:16
  329.2 4.3 collective-permute-start.10
  335.6 65.0 %collective-permute-done.10 = bf16[128,6144]{1,0:T(8,128)(2,1)} collective-permute-done((bf16[128,6144]{1,0:T(8,128)(2,1)S(1)}, bf16[128,6144]{1,0:T(8,128)(2,1)}, u32[]{:S(2)}, u32[]{:S(2)}) %collective-permute-start.10) | collective-permute-done | bytes 1572896 | tf_op jit(solution)/shard_map/ppermute | solution.py:16
  404.6 3.1 fusion.36
  407.6 6.4 %fusion.50 = f32[48,128,128]{1,2,0:T(8,128)} fusion(bf16[48,128,128]{2,1,0:T(8,128)(2,1)} %bitcast.89, bf16[128,48,384]{2,0,1:T(8,128)(2,1)} %copy-done.6, f32[48,128,128]{1,2,0:T(8,128)} %get-tuple-element.10, f32[48,128]{1,0:T(8,128)S(1)} %get-tuple-element.9, pred[128,128]{0,1:T(8,128)(4,1)S(1)} %fusion.76), kind=kOutput, calls=%fused_computation.72 | convolution fusion | flops 405798912 | bytes 9478144 | tf_op jit(solution)/shard_map/thd,hcd->thc/dot_general | solution.py:53
  414.1 3.5 copy.25
  417.6 3.5 fusion.25
  421.1 6.0 %fusion.41 = f32[48,128,128]{1,2,0:T(8,128)} fusion(bf16[48,128,384]{2,1,0:T(8,128)(2,1)} %bitcast.78, f32[128,48,128]{0,2,1:T(8,128)S(1)} %copy-done.17, bf16[128,48,128]{0,2,1:T(8,128)(2,1)} %copy-done.20, bf16[128,48,128]{0,2,1:T(8,128)(2,1)S(1)} %copy-done.19), kind=kOutput, calls=%fused_computation.59 | convolution fusion | flops 614989824 | bytes 14155776 | tf_op jit(solution)/shard_map/transpose(jvp(thc,hce->the))/dot_general | solution.py:39
  427.1 3.5 copy.33
  430.6 2.7 fusion.17
  436.6 5.1 collective-permute-start.6
  443.0 30.6 %collective-permute-done.11 = bf16[128,6144]{1,0:T(8,128)(2,1)} collective-permute-done((bf16[128,6144]{1,0:T(8,128)(2,1)}, bf16[128,6144]{1,0:T(8,128)(2,1)}, u32[]{:S(2)}, u32[]{:S(2)}) %collective-permute-start.11) | collective-permute-done | bytes 1572896 | tf_op jit(solution)/shard_map/ppermute | solution.py:16
  473.6 41.4 %all-reduce.5 = bf16[6144]{0:T(1024)(128)(2,1)S(1)} all-reduce(bf16[6144]{0:T(1024)(128)(2,1)S(1)} %get-tuple-element.5), channel_id=5, replica_groups=mesh['section'=32,'dp'=8] {'dp'}, use_global_device_ids=true, to_apply=%region_11.12.clone | all-reduce | flops 6144 | bytes 24576
  517.9 2.7 copy.57
  521.7 2.7 copy.59
  (96 shorter events, 33.4 us)
Async XLA Ops:
  7.2 208.6 %copy-start.13 = (s32[1,128]{1,0:T(1,128)S(1)}, s32[1,128]{1,0:T(1,128)}, u32[]{:S(2)}) copy-start(s32[1,128]{1,0:T(1,128)} %param.13) | copy-start | bytes 1540
  7.2 249.6 %all-gather.4.cloned.1.call-start = ((), (), s32[]{:S(2)}) async-start(), calls=%async_computation.2 | async-start | bytes 7077888 | tf_op jit(solution)/shard_map/all_gather | solution.py:61
  7.9 507.8 %reduce-scatter.2.cloned.1.call-start = ((), (), s32[]{:S(2)}) async-start(), calls=%async_computation.1 | async-start | bytes 7077888 | tf_op jit(solution)/shard_map/reduce_scatter | solution.py:79
  8.0 3.7 collective-permute-start.1
  11.7 62.5 %collective-permute-start.2 = (bf16[128,6144]{1,0:T(8,128)(2,1)S(1)}, bf16[128,6144]{1,0:T(8,128)(2,1)S(1)}, u32[]{:S(2)}, u32[]{:S(2)}) collective-permute-start(bf16[128,6144]{1,0:T(8,128)(2,1)S(1)} %collective-permute-done.1), channel_id=1, source_target_pairs={{0,16},{8,24},{16,0},{24,8},{32,48},{40,56},{48,32},{56,40},{64,80... | collective-permute-start | bytes 4718600 | tf_op jit(solution)/shard_map/ppermute | solution.py:16
  74.1 34.6 %collective-permute-start.3 = (bf16[128,6144]{1,0:T(8,128)(2,1)S(1)}, bf16[128,6144]{1,0:T(8,128)(2,1)S(1)}, u32[]{:S(2)}, u32[]{:S(2)}) collective-permute-start(bf16[128,6144]{1,0:T(8,128)(2,1)S(1)} %collective-permute-done.2), channel_id=1, source_target_pairs={{0,32},{8,40},{16,48},{24,56},{32,0},{40,8},{48,16},{56,24},{64,96... | collective-permute-start | bytes 4718600 | tf_op jit(solution)/shard_map/ppermute | solution.py:16
  108.8 69.5 %collective-permute-start.4 = (bf16[128,6144]{1,0:T(8,128)(2,1)S(1)}, bf16[128,6144]{1,0:T(8,128)(2,1)S(1)}, u32[]{:S(2)}, u32[]{:S(2)}) collective-permute-start(bf16[128,6144]{1,0:T(8,128)(2,1)S(1)} %collective-permute-done.3), channel_id=1, source_target_pairs={{0,64},{8,72},{16,80},{24,88},{32,96},{40,104},{48,112},{56,120},{... | collective-permute-start | bytes 4718600 | tf_op jit(solution)/shard_map/ppermute | solution.py:16
  113.1 102.7 %collective-permute-start.7 = (bf16[128,6144]{1,0:T(8,128)(2,1)}, bf16[128,6144]{1,0:T(8,128)(2,1)}, u32[]{:S(2)}, u32[]{:S(2)}) collective-permute-start(bf16[128,6144]{1,0:T(8,128)(2,1)} %bitcast.82), channel_id=1, source_target_pairs={{0,8},{8,0},{16,24},{24,16},{32,40},{40,32},{48,56},{56,48},{64,72... | collective-permute-start | bytes 4718600 | tf_op jit(solution)/shard_map/ppermute | solution.py:16
  178.3 74.0 %collective-permute-start.5 = (bf16[128,6144]{1,0:T(8,128)(2,1)S(1)}, bf16[128,6144]{1,0:T(8,128)(2,1)S(1)}, u32[]{:S(2)}, u32[]{:S(2)}) collective-permute-start(bf16[128,6144]{1,0:T(8,128)(2,1)S(1)} %collective-permute-done.4), channel_id=1, source_target_pairs={{0,128},{8,136},{16,144},{24,152},{32,160},{40,168},{48,176},{56,1... | collective-permute-start | bytes 4718600 | tf_op jit(solution)/shard_map/ppermute | solution.py:16
  215.9 78.4 %collective-permute-start.8 = (bf16[128,6144]{1,0:T(8,128)(2,1)}, bf16[128,6144]{1,0:T(8,128)(2,1)}, u32[]{:S(2)}, u32[]{:S(2)}) collective-permute-start(bf16[128,6144]{1,0:T(8,128)(2,1)} %collective-permute-done.7), channel_id=1, source_target_pairs={{0,16},{8,24},{16,0},{24,8},{32,48},{40,56},{48,32},{56,40},{64,80... | collective-permute-start | bytes 4718600 | tf_op jit(solution)/shard_map/ppermute | solution.py:16
  258.3 12.2 %copy-start.8 = (bf16[6144,128]{1,0:T(8,128)(2,1)}, bf16[6144,128]{1,0:T(8,128)(2,1)S(1)}, u32[]{:S(2)}) copy-start(bf16[6144,128]{1,0:T(8,128)(2,1)S(1)} %slice.42) | copy-start | bytes 4718596
  264.0 3.6 copy-start.3
  264.0 6.5 %copy-start.4 = (bf16[128,48,384]{2,0,1:T(8,128)(2,1)}, bf16[128,48,384]{2,0,1:T(8,128)(2,1)S(1)}, u32[]{:S(2)}) copy-start(bf16[128,48,384]{2,0,1:T(8,128)(2,1)S(1)} %get-tuple-element.11) | copy-start | bytes 14155780
  267.6 2.9 copy-start.9
  277.7 3.8 copy-start.5
  277.7 4.7 copy-start.10
  277.7 5.1 copy-start.12
  282.8 5.6 %copy-start.18 = (bf16[128,48,128]{0,2,1:T(8,128)(2,1)}, bf16[128,48,128]{0,2,1:T(8,128)(2,1)S(1)}, u32[]{:S(2)}) copy-start(bf16[128,48,128]{0,2,1:T(8,128)(2,1)S(1)} %fusion.64) | copy-start | bytes 4718596
  288.5 2.5 copy-start.11
  294.3 39.2 %copy-start.2 = (bf16[1,128,6144]{2,1,0:T(8,128)(2,1)S(1)}, bf16[1,128,6144]{2,1,0:T(8,128)(2,1)}, u32[]{:S(2)}) copy-start(bf16[1,128,6144]{2,1,0:T(8,128)(2,1)} %param.7) | copy-start | bytes 4718596
  294.3 34.9 %collective-permute-start.9 = (bf16[128,6144]{1,0:T(8,128)(2,1)}, bf16[128,6144]{1,0:T(8,128)(2,1)S(1)}, u32[]{:S(2)}, u32[]{:S(2)}) collective-permute-start(bf16[128,6144]{1,0:T(8,128)(2,1)} %collective-permute-done.8), channel_id=1, source_target_pairs={{0,32},{8,40},{16,48},{24,56},{32,0},{40,8},{48,16},{56,24},{64,96... | collective-permute-start | bytes 4718600 | tf_op jit(solution)/shard_map/ppermute | solution.py:16
  329.2 71.4 %collective-permute-start.10 = (bf16[128,6144]{1,0:T(8,128)(2,1)S(1)}, bf16[128,6144]{1,0:T(8,128)(2,1)}, u32[]{:S(2)}, u32[]{:S(2)}) collective-permute-start(bf16[128,6144]{1,0:T(8,128)(2,1)S(1)} %collective-permute-done.9), channel_id=1, source_target_pairs={{0,64},{8,72},{16,80},{24,88},{32,96},{40,104},{48,112},{56,120},{... | collective-permute-start | bytes 4718600 | tf_op jit(solution)/shard_map/ppermute | solution.py:16
  333.5 69.1 %slice-start = ((s8[4718592]{0:T(1024)(128)(4,1)}), s8[4194304]{0:T(1024)(128)(4,1)S(1)}, s32[]{:S(2)}) async-start(s8[4718592]{0:T(1024)(128)(4,1)} %bitcast.79), calls=%async_computation.3 | async-start | bytes 8388608
  333.8 68.8 %slice-start.1 = ((s8[4718592]{0:T(1024)(128)(4,1)}), s8[524288]{0:T(1024)(128)(4,1)S(1)}, s32[]{:S(2)}) async-start(s8[4718592]{0:T(1024)(128)(4,1)} %bitcast.79), calls=%async_computation.4 | async-start | bytes 1048576
  400.6 73.0 %collective-permute-start.11 = (bf16[128,6144]{1,0:T(8,128)(2,1)}, bf16[128,6144]{1,0:T(8,128)(2,1)}, u32[]{:S(2)}, u32[]{:S(2)}) collective-permute-start(bf16[128,6144]{1,0:T(8,128)(2,1)} %collective-permute-done.10), channel_id=1, source_target_pairs={{0,128},{8,136},{16,144},{24,152},{32,160},{40,168},{48,176},{56,1... | collective-permute-start | bytes 4718600 | tf_op jit(solution)/shard_map/ppermute | solution.py:16
  404.6 3.1 copy-start.6
  417.6 3.5 copy-start.17
  417.6 3.5 copy-start.19
  421.1 94.6 %collective-permute-start = (bf16[128,6144]{1,0:T(8,128)(2,1)}, bf16[128,6144]{1,0:T(8,128)(2,1)}, u32[]{:S(2)}, u32[]{:S(2)}) collective-permute-start(bf16[128,6144]{1,0:T(8,128)(2,1)} %fusion.25), channel_id=1, source_target_pairs={{248,0},{0,8},{8,16},{16,24},{24,32},{32,40},{40,48},{48,56},{56,6... | collective-permute-start | bytes 4718600 | tf_op jit(solution)/shard_map/ppermute | solution.py:10
  430.6 2.8 copy-start
  435.1 6.6 %copy-start.15 = (u32[256]{0:T(256)S(1)}, u32[256]{0:T(256)}, u32[]{:S(2)}) copy-start(u32[256]{0:T(256)} %constant.47) | copy-start | bytes 3076
  436.6 79.1 %collective-permute-start.6 = (bf16[128,6144]{1,0:T(8,128)(2,1)S(1)}, bf16[128,6144]{1,0:T(8,128)(2,1)S(1)}, u32[]{:S(2)}, u32[]{:S(2)}) collective-permute-start(bf16[128,6144]{1,0:T(8,128)(2,1)S(1)} %fusion.29), channel_id=1, source_target_pairs={{8,0},{16,8},{24,16},{32,24},{40,32},{48,40},{56,48},{64,56},{72,6... | collective-permute-start | bytes 4718600 | tf_op jit(solution)/shard_map/ppermute | solution.py:22
  (5 other events, 8.7 us)
Sparse Core Ops, SparseCore 0:
  9.8 99.6 all-gather.3
  294.4 76.6 reduce-scatter.1
where the time goes:
time: 532 us; the launch traced here: 531 us
  waiting for transfers between devices  329 us (62%)
  blocking collectives  69.8 us (13%)
  matrix products  40.5 us (8%)
  local copies, waits for them, and re-layouts  31.1 us (6%)
  starting transfers between devices  26.9 us (5%)
  other arithmetic  18.7 us (4%)
  between operations  15 us (3%)
    ppermute x10, waiting for transfers between devices, partner(): return lax.ppermute(value, axis, pairs)  328 us
    unnamed x1, blocking collectives  41.4 us
    all_gather x1, blocking collectives, local(): lax.all_gather(gain[0], 'dp', axis=0, tiled=True)  28.4 us
    ppermute x10, starting transfers between devices, partner(): return lax.ppermute(value, axis, pairs)  21.7 us
    unnamed x51, local copies, waits for them, and re-layouts  14.1 us
    dot_general x3, matrix products, section_layer(): jnp.einsum('thd,hcd->thc', attended, out_maps, preferred_element_type=jnp...  13.6 us
    dot_general x4, matrix products, section_layer(): jnp.einsum('thc,hce->the', blocks, in_maps, preferred_element_type=jnp.fl...  11.7 us
  transfers between devices with their start and end apart: 14, of which 8 were waited for; matrix products, arithmetic and copies ran while one was open for 14% of the time, Pallas kernels for 0%

commit v1 on v0

v1 whole, which is shorter than its diff:
```python
import functools

import jax
import jax.numpy as jnp
from jax import lax
from jax.experimental import pallas as pl
from jax.experimental.pallas import tpu as pltpu
from jax.sharding import PartitionSpec as P

MESH = pl.DeviceIdType.MESH
F32 = jnp.float32
BF16 = jnp.bfloat16
NN = (((1,), (0,)), ((), ()))
NT = (((1,), (1,)), ((), ()))
TN = (((0,), (0,)), ((), ()))


def dot(a, b, dims):
    return lax.dot_general(a, b, dims, preferred_element_type=F32)


def kernel(
    n_sec,
    n_dp,
    x_hbm,
    st_hbm,
    gr_hbm,
    w_ref,
    gain_ref,
    fdoc_ref,
    bdoc_ref,
    handed,
    returned,
    parked,
    pgrad,
    ggrad,
    xv,
    sv,
    xf,
    xb,
    gb,
    fwd_out,
    bwd_out,
    dxh,
    dw,
    dg,
    zero,
    pf_own,
    pb_own,
    pf,
    pb,
    sums,
    total,
    loc_sem,
    xf_s,
    xf_r,
    xb_s,
    xb_r,
    gb_s,
    gb_r,
    pf_s,
    pf_r,
    pb_s,
    pb_r,
    ho_s,
    ho_r,
    re_s,
    re_r,
    su_s,
    su_r,
    pa_s,
    pa_r,
):
    tokens, width = x_hbm.shape
    cols = width // n_dp
    hd = w_ref.shape[1] // 4
    heads = cols // hd
    scale = hd ** (-0.5)
    s = lax.axis_index("section")
    g = lax.axis_index("dp")
    mirror = n_sec - 1 - s
    nxt = lax.rem(s + 1, n_sec)
    prv = lax.rem(s + n_sec - 1, n_sec)

    def span(j):
        return pl.ds(pl.multiple_of(j * cols, 128), cols)

    def remote(src, dst, ss, rs, dev):
        return pltpu.make_async_remote_copy(
            src_ref=src,
            dst_ref=dst,
            send_sem=ss,
            recv_sem=rs,
            device_id=dev,
            device_id_type=MESH,
        )

    def each(first, body):
        def step(k, _):
            body(lax.rem(g + k, n_dp))
            return 0

        lax.fori_loop(first, n_dp, step, 0)

    def xf_copy(j):
        return remote(x_hbm.at[:, span(j)], xf.at[g], xf_s.at[j], xf_r.at[g], (s, j))

    def gb_copy(j):
        return remote(gr_hbm.at[:, span(j)], gb.at[g], gb_s.at[j], gb_r.at[g], (s, j))

    def xb_copy(j):
        return remote(st_hbm.at[:, span(j)], xb.at[g], xb_s.at[j], xb_r.at[g], (mirror, j))

    def pf_copy(j):
        return remote(pf_own, pf.at[g], pf_s.at[j], pf_r.at[g], (s, j))

    def pb_copy(j):
        return remote(pb_own, pb.at[g], pb_s.at[j], pb_r.at[g], (mirror, j))

    def ho_copy(j):
        return remote(fwd_out.at[j], handed.at[:, span(g)], ho_s.at[j], ho_r.at[g], (nxt, j))

    def re_copy(j):
        return remote(bwd_out.at[j], returned.at[:, span(g)], re_s.at[j], re_r.at[g], (prv, j))

    def su_copy(j):
        return remote(sums.at[g], sums.at[g], su_s.at[j], su_r.at[g], (s, j))

    def pa_copy():
        return remote(x_hbm, parked, pa_s, pa_r, (mirror, g))

    def xf_in(j):
        return remote(x_hbm.at[:, span(j)], xf.at[j], xf_s.at[j], xf_r.at[j], (s, j))

    def gb_in(j):
        return remote(gr_hbm.at[:, span(j)], gb.at[j], gb_s.at[j], gb_r.at[j], (s, j))

    def xb_in(j):
        return remote(st_hbm.at[:, span(j)], xb.at[j], xb_s.at[j], xb_r.at[j], (mirror, j))

    def pf_in(j):
        return remote(pf_own, pf.at[j], pf_s.at[j], pf_r.at[j], (s, j))

    def pb_in(j):
        return remote(pb_own, pb.at[j], pb_s.at[j], pb_r.at[j], (mirror, j))

    def ho_in(j):
        return remote(fwd_out.at[j], handed.at[:, span(j)], ho_s.at[j], ho_r.at[j], (nxt, j))

    def re_in(j):
        return remote(bwd_out.at[j], returned.at[:, span(j)], re_s.at[j], re_r.at[j], (prv, j))

    def su_in(j):
        return remote(sums.at[j], sums.at[j], su_s.at[j], su_r.at[j], (s, j))

    x_load = pltpu.make_async_copy(x_hbm, xv, loc_sem.at[0])
    s_load = pltpu.make_async_copy(st_hbm, sv, loc_sem.at[1])
    xf_load = pltpu.make_async_copy(x_hbm.at[:, span(g)], xf.at[g], loc_sem.at[2])
    gb_load = pltpu.make_async_copy(gr_hbm.at[:, span(g)], gb.at[g], loc_sem.at[3])
    s_load.start()
    x_load.start()
    xf_load.start()
    gb_load.start()

    barrier = pltpu.get_barrier_semaphore()

    def greet(k, _):
        for section in (mirror, nxt, prv):
            pl.semaphore_signal(barrier, inc=1, device_id=(section, k), device_id_type=MESH)
        return 0

    lax.fori_loop(0, n_dp, greet, 0)
    each(
        1,
        lambda j: pl.semaphore_signal(barrier, inc=1, device_id=(s, j), device_id_type=MESH),
    )
    pl.semaphore_wait(barrier, 4 * n_dp - 1)

    each(0, lambda j: xb_copy(j).start())
    each(1, lambda j: xf_copy(j).start())
    each(1, lambda j: gb_copy(j).start())

    lanes = lax.broadcasted_iota(jnp.int32, (tokens, 128), 1)
    rows8 = lax.broadcasted_iota(jnp.int32, (8, 128), 0)
    chunk = 512

    def statistics(ref):
        def lane_sum(fn):
            def step(c, acc):
                part = ref[:, pl.ds(pl.multiple_of(c * chunk, chunk), chunk)].astype(F32)
                part = fn(part)
                for i in range(chunk // 128):
                    acc = acc + part[:, i * 128 : (i + 1) * 128]
                return acc

            acc = lax.fori_loop(0, width // chunk, step, jnp.zeros((tokens, 128), F32))
            return jnp.sum(acc, axis=1, keepdims=True)

        mean = lane_sum(lambda v: v) / width

        def squared(v):
            return (v - mean) * (v - mean)

        rstd = lax.rsqrt(lane_sum(squared) / width + 1e-05)
        both = jnp.where(lanes == 0, mean, jnp.where(lanes == 1, rstd, 0.0))
        return both.T[0:8, :]

    s_load.wait()
    pb_own[...] = statistics(sv)
    each(0, lambda j: pb_copy(j).start())
    x_load.wait()
    own = statistics(xv)
    own = jnp.where(rows8 == 2, jnp.broadcast_to(fdoc_ref[...].astype(F32), (8, 128)), own)
    own = jnp.where(rows8 == 3, jnp.broadcast_to(bdoc_ref[...].astype(F32), (8, 128)), own)
    pf_own[...] = own
    pf[g] = own
    each(1, lambda j: pf_copy(j).start())

    row_ids = lax.broadcasted_iota(jnp.int32, (tokens, tokens), 0)
    col_ids = lax.broadcasted_iota(jnp.int32, (tokens, tokens), 1)
    causal = col_ids <= row_ids

    def wide(row):
        return jnp.broadcast_to(row, (128, 128)).T

    def allowed_of(docs):
        across = jnp.broadcast_to(docs, (128, 128))
        return causal & (across == across.T)

    def attention(normed, h, allowed):
        w_in = w_ref[h * hd : (h + 1) * hd, : 3 * hd]
        w_out = w_ref[h * hd : (h + 1) * hd, 3 * hd :]
        projected = dot(normed, w_in, NN)
        q = (projected[:, :hd] * scale).astype(BF16)
        k = projected[:, hd : 2 * hd].astype(BF16)
        v = projected[:, 2 * hd :].astype(BF16)
        e = jnp.where(allowed, jnp.exp(dot(q, k, NT)), 0.0)
        p = e * (1.0 / jnp.sum(e, axis=-1, keepdims=True))
        p16 = p.astype(BF16)
        a = dot(p16, v, NN).astype(BF16)
        return w_in, w_out, q, k, v, p, p16, a

    xf_load.wait()
    gb_load.wait()

    def forward(k, _):
        j = lax.rem(g + n_dp - k, n_dp)

        @pl.when(k > 0)
        def _():
            pf_in(j).wait_recv()
            xf_in(j).wait_recv()

        mean = wide(pf[j, 0:1, :])
        rstd = wide(pf[j, 1:2, :])
        allowed = allowed_of(pf[j, 2:3, :])
        for h in range(heads):
            at = slice(h * hd, (h + 1) * hd)
            x = xf[j, :, at].astype(F32)
            normed = ((x - mean) * rstd * gain_ref[:, at].astype(F32)).astype(BF16)
            w_in, w_out, q, key, v, p, p16, a = attention(normed, h, allowed)
            fwd_out[j, :, at] = (x + dot(a, w_out, NT)).astype(BF16)
        ho_copy(j).start()
        return 0

    lax.fori_loop(0, n_dp, forward, 0)

    each(0, lambda j: xb_copy(j).wait_send())
    pa_copy().start()

    dw[...] = jnp.zeros_like(dw)
    dg[...] = jnp.zeros_like(dg)

    group_ids = lax.broadcasted_iota(jnp.int32, (n_dp, 128), 0)

    def backward(k, parts):
        j = lax.rem(g + n_dp - k, n_dp)

        @pl.when(k > 0)
        def _():
            gb_in(j).wait_recv()

        pb_in(j).wait_recv()
        xb_in(j).wait_recv()
        mean = wide(pb[j, 0:1, :])
        rstd = wide(pb[j, 1:2, :])
        allowed = allowed_of(pf[j, 3:4, :])
        first = jnp.zeros((tokens, hd), F32)
        second = jnp.zeros((tokens, hd), F32)
        for h in range(heads):
            at = slice(h * hd, (h + 1) * hd)
            gain = gain_ref[:, at].astype(F32)
            xhat = (xb[j, :, at].astype(F32) - mean) * rstd
            normed = (xhat * gain).astype(BF16)
            w_in, w_out, q, key, v, p, p16, a = attention(normed, h, allowed)
            dy = gb[j, :, at]
            dw[at, 3 * hd :] += dot(dy, a, TN)
            da = dot(dy, w_out, NN).astype(BF16)
            dp = dot(da, v, NT)
            dv = dot(p16, da, TN).astype(BF16)
            ds = (p * (dp - jnp.sum(dp * p, axis=-1, keepdims=True))).astype(BF16)
            dq = (dot(ds, key, NN) * scale).astype(BF16)
            dk = dot(ds, q, TN).astype(BF16)
            dproj = jnp.concatenate([dq, dk, dv], axis=1)
            dw[at, : 3 * hd] += dot(normed, dproj, TN)
            dn = dot(dproj, w_in, NT)
            dg[0:1, at] += jnp.sum(dn * xhat, axis=0, keepdims=True)
            back = dn * gain
            dxh[j, :, at] = back
            first = first + back
            second = second + back * xhat
        here = group_ids == j
        return (
            jnp.where(here, jnp.sum(first.T, axis=0, keepdims=True), parts[0]),
            jnp.where(here, jnp.sum(second.T, axis=0, keepdims=True), parts[1]),
        )

    blank = jnp.zeros((n_dp, 128), F32)
    parts = lax.fori_loop(0, n_dp, backward, (blank, blank))
    sums[g, 0] = parts[0]
    sums[g, 1] = parts[1]

    each(1, lambda j: su_copy(j).start())
    pgrad[...] = (dw[...] * (1.0 / n_dp)).astype(BF16)
    ggrad[...] = (dg[0:1, :] * (1.0 / n_dp)).astype(BF16)
    each(1, lambda j: su_in(j).wait_recv())
    acc = sums[0]
    for i in range(1, n_dp):
        acc = acc + sums[i]
    total[...] = acc * (1.0 / width)

    @pl.when(s > 0)
    def _():
        def finish(k, _):
            j = lax.rem(g + k, n_dp)
            mean = wide(pb[j, 0:1, :])
            rstd = wide(pb[j, 1:2, :])
            here = group_ids == j
            c1 = wide(jnp.sum(jnp.where(here, total[0], 0.0), axis=0, keepdims=True))
            c2 = wide(jnp.sum(jnp.where(here, total[1], 0.0), axis=0, keepdims=True))
            for h in range(heads):
                at = slice(h * hd, (h + 1) * hd)
                xhat = (xb[j, :, at].astype(F32) - mean) * rstd
                back = rstd * (dxh[j, :, at] - c1 - xhat * c2)
                bwd_out[j, :, at] = (gb[j, :, at].astype(F32) + back).astype(BF16)
            re_copy(j).start()
            return 0

        lax.fori_loop(0, n_dp, finish, 0)

    @pl.when(s == n_sec - 1)
    def _():
        zero[...] = jnp.zeros_like(zero)

        def fill(j):
            return pltpu.make_async_copy(zero, returned.at[:, span(j)], re_r.at[j])

        each(0, lambda j: fill(j).start())
        each(0, lambda j: fill(j).wait())

    each(0, lambda j: ho_in(j).wait_recv())

    @pl.when(s < n_sec - 1)
    def _():
        each(0, lambda j: re_in(j).wait_recv())

    pa_copy().wait_recv()
    each(1, lambda j: xf_copy(j).wait_send())
    each(1, lambda j: gb_copy(j).wait_send())
    each(1, lambda j: pf_copy(j).wait_send())
    each(0, lambda j: pb_copy(j).wait_send())
    each(1, lambda j: su_copy(j).wait_send())
    each(0, lambda j: ho_copy(j).wait_send())

    @pl.when(s > 0)
    def _():
        each(0, lambda j: re_copy(j).wait_send())

    pa_copy().wait_send()


def local(n_sec, n_dp, inputs, stash, grad_in, proj, gain, fwd_docs, bwd_docs):
    tokens, width = inputs.shape[1:]
    rows, four = proj.shape[1:]
    blocks = (n_dp, tokens, rows)
    row_sem = pltpu.SemaphoreType.DMA((n_dp,))
    anywhere = pl.BlockSpec(memory_space=pl.ANY)
    vmem = pl.BlockSpec(memory_space=pltpu.VMEM)
    handed, returned, parked, pgrad, ggrad = pl.pallas_call(
        functools.partial(kernel, n_sec, n_dp),
        out_shape=[jax.ShapeDtypeStruct((tokens, width), BF16)] * 3
        + [
            jax.ShapeDtypeStruct((rows, four), BF16),
            jax.ShapeDtypeStruct((1, rows), BF16),
        ],
        in_specs=[anywhere] * 3 + [vmem] * 4,
        out_specs=[anywhere] * 3 + [vmem] * 2,
        scratch_shapes=[
            pltpu.VMEM((tokens, width), BF16),
            pltpu.VMEM((tokens, width), BF16),
            pltpu.VMEM(blocks, BF16),
            pltpu.VMEM(blocks, BF16),
            pltpu.VMEM(blocks, BF16),
            pltpu.VMEM(blocks, BF16),
            pltpu.VMEM(blocks, BF16),
            pltpu.VMEM(blocks, F32),
            pltpu.VMEM((rows, four), F32),
            pltpu.VMEM((8, rows), F32),
            pltpu.VMEM((tokens, rows), BF16),
            pltpu.VMEM((8, 128), F32),
            pltpu.VMEM((8, 128), F32),
            pltpu.VMEM((n_dp, 8, 128), F32),
            pltpu.VMEM((n_dp, 8, 128), F32),
            pltpu.VMEM((n_dp, 2, n_dp, 128), F32),
            pltpu.VMEM((2, n_dp, 128), F32),
            pltpu.SemaphoreType.DMA((4,)),
        ]
        + [row_sem] * 16
        + [pltpu.SemaphoreType.DMA, pltpu.SemaphoreType.DMA],
        compiler_params=pltpu.CompilerParams(
            collective_id=0, has_side_effects=True, vmem_limit_bytes=48 * 1024 * 1024
        ),
    )(inputs[0], stash[0], grad_in[0], proj[0], gain, fwd_docs, bwd_docs)
    return handed[None], returned[None], parked[None], pgrad[None], ggrad


def solution(mesh):
    n_sec, n_dp = mesh.shape["section"], mesh.shape["dp"]
    token_blocks = P("section", "dp", None)
    rows = P("section", "dp")
    return jax.shard_map(
        functools.partial(local, n_sec, n_dp),
        mesh=mesh,
        in_specs=(token_blocks,) * 4 + (rows,) * 3,
        out_specs=(token_blocks,) * 4 + (rows,),
        check_vma=False,
    )
```

time: 532 us -> 207 us (0.39)
  the two profiles are of different devices: /device:TPU:6 before, /device:TPU:27 now
where the time goes in v1:
time: 207 us
  Pallas kernels  197 us (95%)
  local copies, waits for them, and re-layouts  8.84 us (4%)
    pallas_call x1, Pallas kernels, local(): pl.pallas_call(functools.partial(kernel, n_sec, n_dp), out_shape=[jax.Sha...  197 us
    unnamed x15, local copies, waits for them, and re-layouts  8.84 us

profile of v1, /device:TPU:27, one launch (start us, length us, event | category | flops | bytes accessed | tf_op | source)
XLA Modules:
  0.0 206.6 jit_solution(10056542101538566413)
XLA Ops:
  0.6 0.0 copy-start
  0.6 1.1 copy-done
  1.8 0.0 copy-start.1
  1.8 0.7 copy-done.1
  2.5 0.0 copy-start.2
  2.5 0.7 copy-done.2
  3.1 0.0 copy-start.3
  3.1 0.7 copy-done.3
  3.8 197.1 %shard_map.110 = (bf16[128,6144]{1,0:T(8,128)(2,1)S(1)}, bf16[128,6144]{1,0:T(8,128)(2,1)S(1)}, bf16[128,6144]{1,0:T(8,128)(2,1)}, bf16[768,512]{1,0:T(8,128)(2,1)S(1)}, bf16[1,768]{1,0:T(2,128)(2,1)S(1)}) custom-call(bf16[128,6144]{1,0:T(8,128)(2,1)} %bitcast.13, bf16[128,6144]{1,0:T(8,128)(2,1)} %bitcast.14, bf16[128,6144]{1,0:T(8,128)(2,1)} %bitcast.15, ...), custom_call_target="tpu_custom_call" | custom-call | tf_op jit(solution)/shard_map/pallas_call | solution.py:389
  200.8 1.1 copy.17
  202.0 0.0 copy-start.4
  202.0 1.1 copy.18
  203.1 0.8 copy-done.4
  204.0 1.1 copy.19
  205.1 0.9 copy.20
  206.0 0.6 copy.21
Async XLA Ops:
  0.6 1.1 copy-start
  1.8 0.7 copy-start.1
  2.5 0.7 copy-start.2
  3.1 0.7 copy-start.3
  202.0 2.0 copy-start.4

commit v2 on v1

--- a/solution.py
+++ b/solution.py
@@ -10,9 +10,16 @@
 MESH = pl.DeviceIdType.MESH
 F32 = jnp.float32
 BF16 = jnp.bfloat16
+ORDER = {
+    2: ((0, 0), (1, 0)),
+    8: ((0, 0), (0, 1), (1, 3), (0, 3), (1, 1), (0, 2), (1, 0), (1, 2)),
+}
 NN = (((1,), (0,)), ((), ()))
 NT = (((1,), (1,)), ((), ()))
 TN = (((0,), (0,)), ((), ()))
+
+
+AHEAD_NEAR, AHEAD_FAR = 5, 0
 
 
 def dot(a, b, dims):
@@ -42,7 +49,12 @@
     fwd_out,
     bwd_out,
     dxh,
-    dw,
+    dab,
+    nb,
+    vb,
+    pr,
+    ab,
+    dproj,
     dg,
     zero,
     pf_own,
@@ -82,6 +94,10 @@
     nxt = lax.rem(s + 1, n_sec)
     prv = lax.rem(s + n_sec - 1, n_sec)
 
+    z = lax.div(s, 4)
+    near = (lax.rem(z, 4) == 0) | (lax.rem(z, 4) == 3)
+    ahead = jnp.where(near, AHEAD_NEAR, AHEAD_FAR)
+
     def span(j):
         return pl.ds(pl.multiple_of(j * cols, 128), cols)
 
@@ -95,9 +111,25 @@
             device_id_type=MESH,
         )
 
+    ring = n_dp // 2
+    x_lo, y = lax.div(g, ring), lax.rem(g, ring)
+    way = 1 - 2 * lax.rem(s, 2)
+
+    def pick(k, table):
+        value = jnp.int32(table[0])
+        for i in range(1, len(table)):
+            value = jnp.where(k == i, table[i], value)
+        return value
+
+    def peer(k, sign):
+        flip = pick(k, [a for a, _ in ORDER[n_dp]])
+        turn = pick(k, [b for _, b in ORDER[n_dp]])
+        across = x_lo + flip - 2 * x_lo * flip
+        return across * ring + lax.rem(y + sign * turn + ring, ring)
+
     def each(first, body):
         def step(k, _):
-            body(lax.rem(g + k, n_dp))
+            body(peer(k, way))
             return 0
 
         lax.fori_loop(first, n_dp, step, 0)
@@ -126,8 +158,8 @@
     def su_copy(j):
         return remote(sums.at[g], sums.at[g], su_s.at[j], su_r.at[g], (s, j))
 
-    def pa_copy():
-        return remote(x_hbm, parked, pa_s, pa_r, (mirror, g))
+    def pa_copy(j):
+        return remote(x_hbm.at[:, span(j)], parked.at[:, span(j)], pa_s.at[j], pa_r.at[j], (mirror, g))
 
     def xf_in(j):
         return remote(x_hbm.at[:, span(j)], xf.at[j], xf_s.at[j], xf_r.at[j], (s, j))
@@ -176,9 +208,14 @@
     )
     pl.semaphore_wait(barrier, 4 * n_dp - 1)
 
-    each(0, lambda j: xb_copy(j).start())
     each(1, lambda j: xf_copy(j).start())
-    each(1, lambda j: gb_copy(j).start())
+    xb_copy(g).start()
+
+    def both(j):
+        xb_copy(j).start()
+        gb_copy(j).start()
+
+    each(1, both)
 
     lanes = lax.broadcasted_iota(jnp.int32, (tokens, 128), 1)
     rows8 = lax.broadcasted_iota(jnp.int32, (8, 128), 0)
@@ -227,24 +264,26 @@
         across = jnp.broadcast_to(docs, (128, 128))
         return causal & (across == across.T)
 
-    def attention(normed, h, allowed):
-        w_in = w_ref[h * hd : (h + 1) * hd, : 3 * hd]
-        w_out = w_ref[h * hd : (h + 1) * hd, 3 * hd :]
-        projected = dot(normed, w_in, NN)
-        q = (projected[:, :hd] * scale).astype(BF16)
-        k = projected[:, hd : 2 * hd].astype(BF16)
-        v = projected[:, 2 * hd :].astype(BF16)
+    ats = [slice(h * hd, (h + 1) * hd) for h in range(heads)]
+    three = [slice(h * 3 * hd, (h + 1) * 3 * hd) for h in range(heads)]
+
+    def projections(normed, at):
+        projected = dot(normed, w_ref[at, : 3 * hd], NN)
+        return (
+            (projected[:, :hd] * scale).astype(BF16),
+            projected[:, hd : 2 * hd].astype(BF16),
+            projected[:, 2 * hd :].astype(BF16),
+        )
+
+    def probabilities(q, k, allowed):
         e = jnp.where(allowed, jnp.exp(dot(q, k, NT)), 0.0)
-        p = e * (1.0 / jnp.sum(e, axis=-1, keepdims=True))
-        p16 = p.astype(BF16)
-        a = dot(p16, v, NN).astype(BF16)
-        return w_in, w_out, q, k, v, p, p16, a
+        return e * (1.0 / jnp.sum(e, axis=-1, keepdims=True))
 
     xf_load.wait()
     gb_load.wait()
 
     def forward(k, _):
-        j = lax.rem(g + n_dp - k, n_dp)
+        j = peer(k, -way)
 
         @pl.when(k > 0)
         def _():
@@ -254,58 +293,84 @@
         mean = wide(pf[j, 0:1, :])
         rstd = wide(pf[j, 1:2, :])
         allowed = allowed_of(pf[j, 2:3, :])
-        for h in range(heads):
-            at = slice(h * hd, (h + 1) * hd)
+        qkv, probs, attended = [], [], []
+        for at in ats:
             x = xf[j, :, at].astype(F32)
             normed = ((x - mean) * rstd * gain_ref[:, at].astype(F32)).astype(BF16)
-            w_in, w_out, q, key, v, p, p16, a = attention(normed, h, allowed)
-            fwd_out[j, :, at] = (x + dot(a, w_out, NT)).astype(BF16)
+            qkv.append(projections(normed, at))
+        for q, key, v in qkv:
+            probs.append(probabilities(q, key, allowed).astype(BF16))
+        for p, (q, key, v) in zip(probs, qkv):
+            attended.append(dot(p, v, NN).astype(BF16))
+        for at, a in zip(ats, attended):
+            x = xf[j, :, at].astype(F32)
+            fwd_out[j, :, at] = (x + dot(a, w_ref[at, 3 * hd :], NT)).astype(BF16)
         ho_copy(j).start()
         return 0
 
     lax.fori_loop(0, n_dp, forward, 0)
 
-    each(0, lambda j: xb_copy(j).wait_send())
-    pa_copy().start()
-
-    dw[...] = jnp.zeros_like(dw)
-    dg[...] = jnp.zeros_like(dg)
-
-    group_ids = lax.broadcasted_iota(jnp.int32, (n_dp, 128), 0)
-
-    def backward(k, parts):
-        j = lax.rem(g + n_dp - k, n_dp)
+    def park(k, _):
+        j = peer(k, way)
+        xb_copy(j).wait_send()
+
+        @pl.when(k < ahead)
+        def _():
+            pa_copy(j).start()
+        return 0
+
+    lax.fori_loop(0, n_dp, park, 0)
+
+    def early(k, _):
+        j = peer(k, -way)
 
         @pl.when(k > 0)
         def _():
             gb_in(j).wait_recv()
 
+        for at in ats:
+            dab[j, :, at] = dot(gb[j, :, at], w_ref[at, 3 * hd :], NN).astype(BF16)
+        return 0
+
+    lax.fori_loop(0, n_dp, early, 0)
+    dg[...] = jnp.zeros_like(dg)
+    group_ids = lax.broadcasted_iota(jnp.int32, (n_dp, 128), 0)
+
+    def backward(k, parts):
+        j = peer(k, way)
         pb_in(j).wait_recv()
         xb_in(j).wait_recv()
         mean = wide(pb[j, 0:1, :])
         rstd = wide(pb[j, 1:2, :])
         allowed = allowed_of(pf[j, 3:4, :])
+        qkv, probs, dscores = [], [], []
+        for at in ats:
+            gain = gain_ref[:, at].astype(F32)
+            normed = ((xb[j, :, at].astype(F32) - mean) * rstd * gain).astype(BF16)
+            nb[j, :, at] = normed
+            qkv.append(projections(normed, at))
+            vb[j, :, at] = qkv[-1][2]
+        for at, (q, key, v) in zip(ats, qkv):
+            probs.append(probabilities(q, key, allowed))
+            pr[j, :, at] = probs[-1].astype(BF16)
+        for h, at in enumerate(ats):
+            p, p16, da = probs[h], probs[h].astype(BF16), dab[j, :, at]
+            dp = dot(da, qkv[h][2], NT)
+            dscores.append((p * (dp - jnp.sum(dp * p, axis=-1, keepdims=True))).astype(BF16))
+            start = three[h].start
+            dproj[j, :, start + 2 * hd : start + 3 * hd] = dot(p16, da, TN).astype(BF16)
+        for h in range(heads):
+            q, key, v = qkv[h]
+            start = three[h].start
+            dproj[j, :, start : start + hd] = (dot(dscores[h], key, NN) * scale).astype(BF16)
+            dproj[j, :, start + hd : start + 2 * hd] = dot(dscores[h], q, TN).astype(BF16)
         first = jnp.zeros((tokens, hd), F32)
         second = jnp.zeros((tokens, hd), F32)
-        for h in range(heads):
-            at = slice(h * hd, (h + 1) * hd)
-            gain = gain_ref[:, at].astype(F32)
+        for h, at in enumerate(ats):
             xhat = (xb[j, :, at].astype(F32) - mean) * rstd
-            normed = (xhat * gain).astype(BF16)
-            w_in, w_out, q, key, v, p, p16, a = attention(normed, h, allowed)
-            dy = gb[j, :, at]
-            dw[at, 3 * hd :] += dot(dy, a, TN)
-            da = dot(dy, w_out, NN).astype(BF16)
-            dp = dot(da, v, NT)
-            dv = dot(p16, da, TN).astype(BF16)
-            ds = (p * (dp - jnp.sum(dp * p, axis=-1, keepdims=True))).astype(BF16)
-            dq = (dot(ds, key, NN) * scale).astype(BF16)
-            dk = dot(ds, q, TN).astype(BF16)
-            dproj = jnp.concatenate([dq, dk, dv], axis=1)
-            dw[at, : 3 * hd] += dot(normed, dproj, TN)
-            dn = dot(dproj, w_in, NT)
+            dn = dot(dproj[j, :, three[h]], w_ref[at, : 3 * hd], NT)
             dg[0:1, at] += jnp.sum(dn * xhat, axis=0, keepdims=True)
-            back = dn * gain
+            back = dn * gain_ref[:, at].astype(F32)
             dxh[j, :, at] = back
             first = first + back
             second = second + back * xhat
@@ -321,8 +386,6 @@
     sums[g, 1] = parts[1]
 
     each(1, lambda j: su_copy(j).start())
-    pgrad[...] = (dw[...] * (1.0 / n_dp)).astype(BF16)
-    ggrad[...] = (dg[0:1, :] * (1.0 / n_dp)).astype(BF16)
     each(1, lambda j: su_in(j).wait_recv())
     acc = sums[0]
     for i in range(1, n_dp):
@@ -332,7 +395,7 @@
     @pl.when(s > 0)
     def _():
         def finish(k, _):
-            j = lax.rem(g + k, n_dp)
+            j = peer(k, way)
             mean = wide(pb[j, 0:1, :])
             rstd = wide(pb[j, 1:2, :])
             here = group_ids == j
@@ -344,9 +407,22 @@
                 back = rstd * (dxh[j, :, at] - c1 - xhat * c2)
                 bwd_out[j, :, at] = (gb[j, :, at].astype(F32) + back).astype(BF16)
             re_copy(j).start()
+
+            @pl.when(k >= ahead)
+            def _():
+                pa_copy(j).start()
+
             return 0
 
         lax.fori_loop(0, n_dp, finish, 0)
+
+    @pl.when(s == 0)
+    def _():
+        def rest(k, _):
+            pa_copy(peer(k, way)).start()
+            return 0
+
+        lax.fori_loop(ahead, n_dp, rest, 0)
 
     @pl.when(s == n_sec - 1)
     def _():
@@ -358,13 +434,29 @@
         each(0, lambda j: fill(j).start())
         each(0, lambda j: fill(j).wait())
 
+    def attend(j, _):
+        for at in ats:
+            ab[j, :, at] = dot(pr[j, :, at], vb[j, :, at], NN).astype(BF16)
+        return 0
+
+    lax.fori_loop(0, n_dp, attend, 0)
+    every = n_dp * tokens
+    for h, at in enumerate(ats):
+        normed = nb[:, :, at].reshape(every, hd)
+        into = dot(normed, dproj[:, :, three[h]].reshape(every, 3 * hd), TN)
+        pgrad[at, : 3 * hd] = (into * (1.0 / n_dp)).astype(BF16)
+        dy = gb[:, :, at].reshape(every, hd)
+        out = dot(dy, ab[:, :, at].reshape(every, hd), TN)
+        pgrad[at, 3 * hd :] = (out * (1.0 / n_dp)).astype(BF16)
+    ggrad[...] = (dg[0:1, :] * (1.0 / n_dp)).astype(BF16)
+
     each(0, lambda j: ho_in(j).wait_recv())
 
     @pl.when(s < n_sec - 1)
     def _():
         each(0, lambda j: re_in(j).wait_recv())
 
-    pa_copy().wait_recv()
+    each(0, lambda j: pa_copy(j).wait_recv())
     each(1, lambda j: xf_copy(j).wait_send())
     each(1, lambda j: gb_copy(j).wait_send())
     each(1, lambda j: pf_copy(j).wait_send())
@@ -376,7 +468,7 @@
     def _():
         each(0, lambda j: re_copy(j).wait_send())
 
-    pa_copy().wait_send()
+    each(0, lambda j: pa_copy(j).wait_send())
 
 
 def local(n_sec, n_dp, inputs, stash, grad_in, proj, gain, fwd_docs, bwd_docs):
@@ -404,7 +496,12 @@
             pltpu.VMEM(blocks, BF16),
             pltpu.VMEM(blocks, BF16),
             pltpu.VMEM(blocks, F32),
-            pltpu.VMEM((rows, four), F32),
+            pltpu.VMEM(blocks, BF16),
+            pltpu.VMEM(blocks, BF16),
+            pltpu.VMEM(blocks, BF16),
+            pltpu.VMEM(blocks, BF16),
+            pltpu.VMEM(blocks, BF16),
+            pltpu.VMEM((n_dp, tokens, 3 * rows), BF16),
             pltpu.VMEM((8, rows), F32),
             pltpu.VMEM((tokens, rows), BF16),
             pltpu.VMEM((8, 128), F32),
@@ -415,8 +512,7 @@
             pltpu.VMEM((2, n_dp, 128), F32),
             pltpu.SemaphoreType.DMA((4,)),
         ]
-        + [row_sem] * 16
-        + [pltpu.SemaphoreType.DMA, pltpu.SemaphoreType.DMA],
+        + [row_sem] * 18,
         compiler_params=pltpu.CompilerParams(
             collective_id=0, has_side_effects=True, vmem_limit_bytes=48 * 1024 * 1024
         ),

time: 207 us -> 184 us (0.89)
  the two profiles are of different devices: /device:TPU:27 before, /device:TPU:103 now
where the time goes in v2:
time: 184 us; the launch traced here: 183 us
  Pallas kernels  174 us (95%)
  local copies, waits for them, and re-layouts  8.84 us (5%)
    pallas_call x1, Pallas kernels, local(): pl.pallas_call(functools.partial(kernel, n_sec, n_dp), out_shape=[jax.Sha...  174 us
    unnamed x15, local copies, waits for them, and re-layouts  8.84 us

profile of v2, /device:TPU:103, one launch (start us, length us, event | category | flops | bytes accessed | tf_op | source)
XLA Modules:
  0.0 183.5 jit_solution(4350672940077789713)
XLA Ops:
  0.6 0.0 copy-start
  0.6 1.1 copy-done
  1.8 0.0 copy-start.1
  1.8 0.7 copy-done.1
  2.5 0.0 copy-start.2
  2.5 0.7 copy-done.2
  3.1 0.0 copy-start.3
  3.1 0.7 copy-done.3
  3.8 174.0 %shard_map.110 = (bf16[128,6144]{1,0:T(8,128)(2,1)S(1)}, bf16[128,6144]{1,0:T(8,128)(2,1)S(1)}, bf16[128,6144]{1,0:T(8,128)(2,1)}, bf16[768,512]{1,0:T(8,128)(2,1)S(1)}, bf16[1,768]{1,0:T(2,128)(2,1)S(1)}) custom-call(bf16[128,6144]{1,0:T(8,128)(2,1)} %bitcast.13, bf16[128,6144]{1,0:T(8,128)(2,1)} %bitcast.14, bf16[128,6144]{1,0:T(8,128)(2,1)} %bitcast.15, ...), custom_call_target="tpu_custom_call" | custom-call | tf_op jit(solution)/shard_map/pallas_call | solution.py:481
  177.7 1.1 copy.17
  178.9 0.0 copy-start.4
  178.9 1.1 copy.18
  180.0 0.8 copy-done.4
  180.9 1.1 copy.19
  182.0 0.9 copy.20
  182.9 0.6 copy.21
Async XLA Ops:
  0.6 1.1 copy-start
  1.8 0.7 copy-start.1
  2.5 0.7 copy-start.2
  3.1 0.7 copy-start.3
  178.9 2.0 %copy-start.4 = (bf16[128,6144]{1,0:T(8,128)(2,1)S(1)}, bf16[128,6144]{1,0:T(8,128)(2,1)}, u32[]{:S(2)}) copy-start(bf16[128,6144]{1,0:T(8,128)(2,1)} %get-tuple-element.12) | copy-start | bytes 4718596

commit v3 on v2

--- a/solution.py
+++ b/solution.py
@@ -14,12 +14,10 @@
     2: ((0, 0), (1, 0)),
     8: ((0, 0), (0, 1), (1, 3), (0, 3), (1, 1), (0, 2), (1, 0), (1, 2)),
 }
+FIRST = {2: 0, 8: 6}
 NN = (((1,), (0,)), ((), ()))
 NT = (((1,), (1,)), ((), ()))
 TN = (((0,), (0,)), ((), ()))
-
-
-AHEAD_NEAR, AHEAD_FAR = 5, 0
 
 
 def dot(a, b, dims):
@@ -82,6 +80,9 @@
     su_r,
     pa_s,
     pa_r,
+    vi_s,
+    vi_r,
+    via,
 ):
     tokens, width = x_hbm.shape
     cols = width // n_dp
@@ -96,7 +97,17 @@
 
     z = lax.div(s, 4)
     near = (lax.rem(z, 4) == 0) | (lax.rem(z, 4) == 3)
-    ahead = jnp.where(near, AHEAD_NEAR, AHEAD_FAR)
+    half = n_sec // 2
+    h_from = lax.rem(s, half) == half - 1
+    h_via = lax.rem(s, half) == half - 3
+    h_to = lax.rem(s, half) == 0
+    r_from, r_via, r_to = s == half, s == half + 2, s == half - 1
+
+    ahead = jnp.where(near & (lax.rem(s, 4) != 0), n_dp, 0)
+    ahead = jnp.where(lax.rem(s, half) == 4, 3, ahead)
+
+    def detour(j):
+        return lax.rem(g + n_dp - j, ring) == 0
 
     def span(j):
         return pl.ds(pl.multiple_of(j * cols, 128), cols)
@@ -155,6 +166,38 @@
     def re_copy(j):
         return remote(bwd_out.at[j], returned.at[:, span(g)], re_s.at[j], re_r.at[g], (prv, j))
 
+    def ho_first(j):
+        return remote(fwd_out.at[j], via.at[g], ho_s.at[j], vi_r.at[g], (s - 2, j))
+
+    def ho_second(j):
+        return remote(via.at[j], handed.at[:, span(j)], vi_s.at[j], ho_r.at[j], (lax.rem(s + 3, n_sec), g))
+
+    def re_first(j):
+        return remote(bwd_out.at[j], via.at[g], re_s.at[j], vi_r.at[g], (s + 2, j))
+
+    def re_second(j):
+        return remote(via.at[j], returned.at[:, span(j)], vi_s.at[j], re_r.at[j], (s - 3, g))
+
+    def vi_in(j):
+        return remote(fwd_out.at[j], via.at[j], ho_s.at[j], vi_r.at[j], (s, j))
+
+    def forward_by(second):
+        def step(j):
+            @pl.when(detour(j))
+            def _():
+                vi_in(j).wait_recv()
+                second(j).start()
+
+        each(0, step)
+
+    def forwarded(second):
+        def step(j):
+            @pl.when(detour(j))
+            def _():
+                second(j).wait_send()
+
+        each(0, step)
+
     def su_copy(j):
         return remote(sums.at[g], sums.at[g], su_s.at[j], su_r.at[g], (s, j))
 
@@ -206,7 +249,32 @@
         1,
         lambda j: pl.semaphore_signal(barrier, inc=1, device_id=(s, j), device_id_type=MESH),
     )
-    pl.semaphore_wait(barrier, 4 * n_dp - 1)
+
+    def greet_row(section):
+        def one(k, _):
+            pl.semaphore_signal(barrier, inc=1, device_id=(section, k), device_id_type=MESH)
+            return 0
+
+        lax.fori_loop(0, n_dp, one, 0)
+
+    def greet_one(section):
+        pl.semaphore_signal(barrier, inc=1, device_id=(section, g), device_id_type=MESH)
+
+    pl.when(h_from)(lambda: greet_row(s - 2))
+    pl.when(h_via)(lambda: greet_row(s + 2))
+    pl.when(h_via)(lambda: greet_one(lax.rem(s + 3, n_sec)))
+    pl.when(h_to)(lambda: greet_one(lax.rem(s + n_sec - 3, n_sec)))
+    pl.when(r_from)(lambda: greet_row(s + 2))
+    pl.when(r_via)(lambda: greet_row(s - 2))
+    pl.when(r_via)(lambda: greet_one(s - 3))
+    pl.when(r_to)(lambda: greet_one(s + 3))
+
+    def count(*roles):
+        return sum(role.astype(jnp.int32) for role in roles)
+
+    rows_met = count(h_from, h_via, r_from, r_via)
+    ones_met = count(h_via, h_to, r_via, r_to)
+    pl.semaphore_wait(barrier, 4 * n_dp - 1 + n_dp * rows_met + ones_met)
 
     each(1, lambda j: xf_copy(j).start())
     xb_copy(g).start()
@@ -305,7 +373,16 @@
         for at, a in zip(ats, attended):
             x = xf[j, :, at].astype(F32)
             fwd_out[j, :, at] = (x + dot(a, w_ref[at, 3 * hd :], NT)).astype(BF16)
-        ho_copy(j).start()
+        aside = h_from & detour(j)
+
+        @pl.when(aside)
+        def _():
+            ho_first(j).start()
+
+        @pl.when(jnp.logical_not(aside))
+        def _():
+            ho_copy(j).start()
+
         return 0
 
     lax.fori_loop(0, n_dp, forward, 0)
@@ -386,6 +463,11 @@
     sums[g, 1] = parts[1]
 
     each(1, lambda j: su_copy(j).start())
+
+    @pl.when(h_via)
+    def _():
+        forward_by(ho_second)
+
     each(1, lambda j: su_in(j).wait_recv())
     acc = sums[0]
     for i in range(1, n_dp):
@@ -395,7 +477,7 @@
     @pl.when(s > 0)
     def _():
         def finish(k, _):
-            j = peer(k, way)
+            j = peer(lax.rem(k + FIRST[n_dp], n_dp), way)
             mean = wide(pb[j, 0:1, :])
             rstd = wide(pb[j, 1:2, :])
             here = group_ids == j
@@ -406,23 +488,29 @@
                 xhat = (xb[j, :, at].astype(F32) - mean) * rstd
                 back = rstd * (dxh[j, :, at] - c1 - xhat * c2)
                 bwd_out[j, :, at] = (gb[j, :, at].astype(F32) + back).astype(BF16)
-            re_copy(j).start()
-
-            @pl.when(k >= ahead)
+            aside = r_from & detour(j)
+
+            @pl.when(aside)
             def _():
-                pa_copy(j).start()
+                re_first(j).start()
+
+            @pl.when(jnp.logical_not(aside))
+            def _():
+                re_copy(j).start()
 
             return 0
 
         lax.fori_loop(0, n_dp, finish, 0)
 
-    @pl.when(s == 0)
-    def _():
-        def rest(k, _):
-            pa_copy(peer(k, way)).start()
-            return 0
-
-        lax.fori_loop(ahead, n_dp, rest, 0)
+    @pl.when(r_via)
+    def _():
+        forward_by(re_second)
+
+    def rest(k, _):
+        pa_copy(peer(k, way)).start()
+        return 0
+
+    lax.fori_loop(ahead, n_dp, rest, 0)
 
     @pl.when(s == n_sec - 1)
     def _():
@@ -457,6 +545,14 @@
         each(0, lambda j: re_in(j).wait_recv())
 
     each(0, lambda j: pa_copy(j).wait_recv())
+    @pl.when(h_via)
+    def _():
+        forwarded(ho_second)
+
+    @pl.when(r_via)
+    def _():
+        forwarded(re_second)
+
     each(1, lambda j: xf_copy(j).wait_send())
     each(1, lambda j: gb_copy(j).wait_send())
     each(1, lambda j: pf_copy(j).wait_send())
@@ -512,7 +608,8 @@
             pltpu.VMEM((2, n_dp, 128), F32),
             pltpu.SemaphoreType.DMA((4,)),
         ]
-        + [row_sem] * 18,
+        + [row_sem] * 20
+        + [pltpu.VMEM(blocks, BF16)],
         compiler_params=pltpu.CompilerParams(
             collective_id=0, has_side_effects=True, vmem_limit_bytes=48 * 1024 * 1024
         ),

time: 184 us -> 178 us (0.967)
  Pallas kernels: 174 us -> 168 us
    pallas_call x1, Pallas kernels: 174 us -> 168 us  [local(): pl.pallas_call(functools.partial(kernel, n_sec, n_dp), out_shape=[jax.Sha...]
where the time goes in v3:
time: 178 us
  Pallas kernels  168 us (94%)
  local copies, waits for them, and re-layouts  8.84 us (5%)
    pallas_call x1, Pallas kernels, local(): pl.pallas_call(functools.partial(kernel, n_sec, n_dp), out_shape=[jax.Sha...  168 us
    unnamed x15, local copies, waits for them, and re-layouts  8.84 us

profile of v3, /device:TPU:103, one launch (start us, length us, event | category | flops | bytes accessed | tf_op | source)
XLA Modules:
  0.0 178.0 jit_solution(3708855389216293113)
XLA Ops:
  0.6 0.0 copy-start
  0.6 1.1 copy-done
  1.8 0.0 copy-start.1
  1.8 0.7 copy-done.1
  2.5 0.0 copy-start.2
  2.5 0.7 copy-done.2
  3.1 0.0 copy-start.3
  3.1 0.7 copy-done.3
  3.8 168.5 %shard_map.110 = (bf16[128,6144]{1,0:T(8,128)(2,1)S(1)}, bf16[128,6144]{1,0:T(8,128)(2,1)S(1)}, bf16[128,6144]{1,0:T(8,128)(2,1)}, bf16[768,512]{1,0:T(8,128)(2,1)S(1)}, bf16[1,768]{1,0:T(2,128)(2,1)S(1)}) custom-call(bf16[128,6144]{1,0:T(8,128)(2,1)} %bitcast.13, bf16[128,6144]{1,0:T(8,128)(2,1)} %bitcast.14, bf16[128,6144]{1,0:T(8,128)(2,1)} %bitcast.15, ...), custom_call_target="tpu_custom_call" | custom-call | tf_op jit(solution)/shard_map/pallas_call | solution.py:577
  172.2 1.1 copy.17
  173.4 0.0 copy-start.4
  173.4 1.1 copy.18
  174.5 0.8 copy-done.4
  175.4 1.1 copy.19
  176.5 0.9 copy.20
  177.4 0.6 copy.21
Async XLA Ops:
  0.6 1.1 copy-start
  1.8 0.7 copy-start.1
  2.5 0.7 copy-start.2
  3.1 0.7 copy-start.3
  173.4 2.0 %copy-start.4 = (bf16[128,6144]{1,0:T(8,128)(2,1)S(1)}, bf16[128,6144]{1,0:T(8,128)(2,1)}, u32[]{:S(2)}) copy-start(bf16[128,6144]{1,0:T(8,128)(2,1)} %get-tuple-element.12) | copy-start | bytes 4718596

commit v4 on v3

--- a/solution.py
+++ b/solution.py
@@ -103,7 +103,7 @@
     h_to = lax.rem(s, half) == 0
     r_from, r_via, r_to = s == half, s == half + 2, s == half - 1
 
-    ahead = jnp.where(near & (lax.rem(s, 4) != 0), n_dp, 0)
+    ahead = jnp.where(near & ((lax.rem(s, 4) != 0) | (s == 0)), n_dp, 0)
     ahead = jnp.where(lax.rem(s, half) == 4, 3, ahead)
 
     def detour(j):
@@ -276,14 +276,9 @@
     ones_met = count(h_via, h_to, r_via, r_to)
     pl.semaphore_wait(barrier, 4 * n_dp - 1 + n_dp * rows_met + ones_met)
 
+    each(0, lambda j: xb_copy(j).start())
     each(1, lambda j: xf_copy(j).start())
-    xb_copy(g).start()
-
-    def both(j):
-        xb_copy(j).start()
-        gb_copy(j).start()
-
-    each(1, both)
+    each(1, lambda j: gb_copy(j).start())
 
     lanes = lax.broadcasted_iota(jnp.int32, (tokens, 128), 1)
     rows8 = lax.broadcasted_iota(jnp.int32, (8, 128), 0)

time: 178 us -> 178 us (level)
  no operation moved by 1% of the time
where the time goes in v4:
time: 178 us
  Pallas kernels  168 us (94%)
  local copies, waits for them, and re-layouts  8.84 us (5%)
    pallas_call x1, Pallas kernels, local(): pl.pallas_call(functools.partial(kernel, n_sec, n_dp), out_shape=[jax.Sha...  168 us
    unnamed x15, local copies, waits for them, and re-layouts  8.84 us

profile of v4, /device:TPU:103, one launch (start us, length us, event | category | flops | bytes accessed | tf_op | source)
XLA Modules:
  0.0 178.0 jit_solution(14839896064603362897)
XLA Ops:
  0.6 0.0 copy-start
  0.6 1.1 copy-done
  1.8 0.0 copy-start.1
  1.8 0.7 copy-done.1
  2.5 0.0 copy-start.2
  2.5 0.7 copy-done.2
  3.1 0.0 copy-start.3
  3.1 0.7 copy-done.3
  3.8 168.5 %shard_map.110 = (bf16[128,6144]{1,0:T(8,128)(2,1)S(1)}, bf16[128,6144]{1,0:T(8,128)(2,1)S(1)}, bf16[128,6144]{1,0:T(8,128)(2,1)}, bf16[768,512]{1,0:T(8,128)(2,1)S(1)}, bf16[1,768]{1,0:T(2,128)(2,1)S(1)}) custom-call(bf16[128,6144]{1,0:T(8,128)(2,1)} %bitcast.13, bf16[128,6144]{1,0:T(8,128)(2,1)} %bitcast.14, bf16[128,6144]{1,0:T(8,128)(2,1)} %bitcast.15, ...), custom_call_target="tpu_custom_call" | custom-call | tf_op jit(solution)/shard_map/pallas_call | solution.py:572
  172.3 1.1 copy.17
  173.4 0.0 copy-start.4
  173.4 1.1 copy.18
  174.5 0.8 copy-done.4
  175.4 1.1 copy.19
  176.5 0.9 copy.20
  177.4 0.6 copy.21
Async XLA Ops:
  0.6 1.1 copy-start
  1.8 0.7 copy-start.1
  2.5 0.7 copy-start.2
  3.1 0.7 copy-start.3
  173.4 2.0 %copy-start.4 = (bf16[128,6144]{1,0:T(8,128)(2,1)S(1)}, bf16[128,6144]{1,0:T(8,128)(2,1)}, u32[]{:S(2)}) copy-start(bf16[128,6144]{1,0:T(8,128)(2,1)} %get-tuple-element.12) | copy-start | bytes 4718596
